TPU v7x, 512 devices: a whole 4x8x8 slice. The times are simulated.
512 devices in a mesh: outer: 128 (over z, y, core), inner: 4 (over x).
Axes of the slice: x: 4, y: 8, z: 8, core: 2. Of those that a mesh axis runs over, the one named last changes fastest.
Arguments:
- query_states: bfloat16 [65536, 4096], P(('outer', 'inner')), may hold values from -6 to 6
- key_states: bfloat16 [65536, 4096], P(('outer', 'inner')), may hold values from -6 to 6
- value_states: bfloat16 [65536, 4096], P(('outer', 'inner')), may hold values from -6 to 6
- doc_lengths: int32 [128], replicated, may hold values from 1 to 1024, 65536 in all
- slopes: float32 [32], replicated, may hold values from 0.00024414062 to 0.0625
Outputs:
- attended: bfloat16 [65536, 4096], P(('outer', 'inner'))
Inputs may be any that keep to these rules, and one draw needn't show every extreme that they name: `doc_lengths`: the lengths add up to 65536; the longest is exactly 1024.
All inputs are finite; a program needn't handle non-finite values.
Results may differ from a plain program's by a relative error of at most 0.0045.
Values may be sent and summed in bfloat16 or wider, within the bound.
No kernel may reach another device: no remote copies, remote signals or barrier semaphores. Data moves between devices by JAX's collectives and lax.ppermute only.
A program may use at most 64 MiB of HBM per device.

v0:
```python
import math
import jax
import jax.numpy as jnp
from jax import lax
from jax.sharding import PartitionSpec as P

SPAN = 2
NEG_FILL = -1e30


def shifted(value, axis, steps):
    count = lax.axis_size(axis)
    first, last = (max(0, -steps), min(count, count - steps))
    return lax.ppermute(value, axis, [(source, source + steps) for source in range(first, last)])


def document_of(positions, doc_lengths):
    boundary = jnp.cumsum(doc_lengths)
    return jnp.sum((boundary[None, :] <= positions[:, None]).astype(jnp.int32), axis=1)


def empty_status(row_count, head_count, head_width):
    return (
        jnp.full((row_count, head_count), NEG_FILL, jnp.float32),
        jnp.zeros((row_count, head_count), jnp.float32),
        jnp.zeros((row_count, head_count, head_width), jnp.float32),
    )


def attend_block(status, query_parts, key_slab, value_slab, key_pos, key_doc, slopes):
    query_rows, query_pos, query_doc = query_parts
    allowed = (query_doc[:, None] == key_doc[None, :]) & (key_pos[None, :] <= query_pos[:, None])

    def update(current):
        running_max, row_total, weighted_sum = current
        scores = jnp.einsum(
            "qhd,khd->qhk", query_rows, key_slab, preferred_element_type=jnp.float32
        )
        scores = scores * (1.0 / math.sqrt(query_rows.shape[-1]))
        distance = (query_pos[:, None] - key_pos[None, :]).astype(jnp.float32)
        scores = scores - slopes[None, :, None] * distance[:, None, :]
        scores = jnp.where(allowed[:, None, :], scores, NEG_FILL)
        new_max = jnp.maximum(running_max, jnp.max(scores, axis=-1))
        weights = jnp.where(allowed[:, None, :], jnp.exp(scores - new_max[:, :, None]), 0.0)
        rescale = jnp.exp(running_max - new_max)
        row_total = row_total * rescale + jnp.sum(weights, axis=-1)
        products = jnp.einsum(
            "qhk,khd->qhd",
            weights.astype(jnp.bfloat16),
            value_slab,
            preferred_element_type=jnp.float32,
        )
        weighted_sum = weighted_sum * rescale[:, :, None] + products
        return (new_max, row_total, weighted_sum)

    def unchanged(current):
        return current

    return lax.cond(jnp.any(allowed), update, unchanged, status)


def attend_keys(status, query_parts, key_slab, value_slab, key_pos, slopes, doc_lengths):
    key_doc = document_of(key_pos, doc_lengths)
    key_count = key_slab.shape[0]
    slab_rows = 256
    pieces = key_count // slab_rows
    stacked = (
        key_slab.reshape((pieces, slab_rows) + key_slab.shape[1:]),
        value_slab.reshape((pieces, slab_rows) + value_slab.shape[1:]),
        key_pos.reshape(pieces, slab_rows),
        key_doc.reshape(pieces, slab_rows),
    )

    def scan_step(current, portion):
        return (
            attend_block(
                current, query_parts, portion[0], portion[1], portion[2], portion[3], slopes
            ),
            None,
        )

    result, unused = lax.scan(scan_step, status, stacked)
    return result


def combine(first_status, second_status):
    new_max = jnp.maximum(first_status[0], second_status[0])
    left_scale = jnp.exp(first_status[0] - new_max)
    right_scale = jnp.exp(second_status[0] - new_max)
    return (
        new_max,
        first_status[1] * left_scale + second_status[1] * right_scale,
        first_status[2] * left_scale[:, :, None] + second_status[2] * right_scale[:, :, None],
    )


def queries_from_later(query_rows, hops_back):
    return shifted(query_rows, "outer", -hops_back)


def partials_home(status, hops_back):
    running_max, row_total, weighted_sum = status
    moved_max, moved_total, moved_sum = shifted(
        (running_max, row_total, weighted_sum), "outer", hops_back
    )
    return (jnp.where(moved_total > 0.0, moved_max, NEG_FILL), moved_total, moved_sum)


def rows_of(status, slot_index, row_count):
    return tuple(
        (member[slot_index * row_count : (slot_index + 1) * row_count] for member in status)
    )


def bring_home(status, row_count, span_count):
    own_status = rows_of(status, 0, row_count)
    distant = [rows_of(status, hops_back, row_count) for hops_back in range(1, span_count + 1)]
    merged = own_status
    for hops_back in range(1, span_count + 1):
        merged = combine(merged, partials_home(distant[hops_back - 1], hops_back))
    return merged


def with_later_queries(own_rows, own_pos, group_rows, span_count, doc_lengths):
    rows_list = [own_rows]
    pos_list = [own_pos]
    for hops_back in range(1, span_count + 1):
        rows_list.append(queries_from_later(own_rows, hops_back))
        pos_list.append(own_pos + hops_back * group_rows)
    all_pos = jnp.concatenate(pos_list)
    return (jnp.concatenate(rows_list, axis=0), all_pos, document_of(all_pos, doc_lengths))


def normalize(status):
    return (status[2] / status[1][:, :, None]).astype(jnp.bfloat16)


def per_device(query_states, key_states, value_states, doc_lengths, slopes):
    rows_dev = query_states.shape[0]
    head_count = slopes.shape[0]
    head_width = query_states.shape[1] // head_count
    inner_count = lax.axis_size("inner")
    group_index = lax.axis_index("outer")
    inner_index = lax.axis_index("inner")
    group_rows = rows_dev * inner_count
    group_start = group_index * group_rows
    own_queries = query_states.reshape(rows_dev, head_count, head_width)
    own_pos = group_start + inner_index * rows_dev + jnp.arange(rows_dev, dtype=jnp.int32)
    query_parts = with_later_queries(own_queries, own_pos, group_rows, SPAN, doc_lengths)
    status = empty_status(query_parts[0].shape[0], head_count, head_width)
    portions = (
        lax.all_gather(
            key_states.reshape(rows_dev, head_count, head_width), "inner", axis=0, tiled=True
        ),
        lax.all_gather(
            value_states.reshape(rows_dev, head_count, head_width), "inner", axis=0, tiled=True
        ),
    )
    key_pos = group_start + jnp.arange(portions[0].shape[0], dtype=jnp.int32)
    status = attend_keys(
        status, query_parts, portions[0], portions[1], key_pos, slopes, doc_lengths
    )
    combined = bring_home(status, rows_dev, SPAN)
    return normalize(combined).reshape(rows_dev, head_count * head_width)


def solution(mesh):
    placed = (
        P(("outer", "inner"), None),
        P(("outer", "inner"), None),
        P(("outer", "inner"), None),
        P(),
        P(),
    )
    return jax.shard_map(
        per_device,
        mesh=mesh,
        in_specs=placed,
        out_specs=P(("outer", "inner"), None),
        check_vma=False,
    )
```

profile of v0, /device:TPU:256, one launch (start us, length us, event | category | flops | bytes accessed | tf_op | source)
XLA Modules:
  0.0 273.0 jit_solution(12478321590578903642)
XLA Ops:
  6.5 2.5 copy.32
  9.1 2.4 copy.33
  12.3 3.9 %collective-permute-start = (bf16[128,32,128]{0,2,1:T(8,128)(2,1)S(1)}, bf16[128,32,128]{0,2,1:T(8,128)(2,1)S(1)}, u32[]{:S(2)}, u32[]{:S(2)}) collective-permute-start(bf16[128,32,128]{0,2,1:T(8,128)(2,1)S(1)} %bitcast.49), channel_id=1, source_target_pairs={{4,0},{8,4},{12,8},{16,12},{20,16},{24,20},{28,24},{32,28},{36,32}... | collective-permute-start | bytes 3145736 | tf_op jit(solution)/shard_map/ppermute | solution.py:14
  16.2 3.3 %collective-permute-start.1 = (bf16[128,32,128]{0,2,1:T(8,128)(2,1)S(1)}, bf16[128,32,128]{0,2,1:T(8,128)(2,1)}, u32[]{:S(2)}, u32[]{:S(2)}) collective-permute-start(bf16[128,32,128]{0,2,1:T(8,128)(2,1)S(1)} %bitcast.50), channel_id=1, source_target_pairs={{8,0},{12,4},{16,8},{20,12},{24,16},{28,20},{32,24},{36,28},{40,32... | collective-permute-start | bytes 3145736 | tf_op jit(solution)/shard_map/ppermute | solution.py:14
  20.4 17.2 %collective-permute-done = bf16[128,32,128]{0,2,1:T(8,128)(2,1)S(1)} collective-permute-done((bf16[128,32,128]{0,2,1:T(8,128)(2,1)S(1)}, bf16[128,32,128]{0,2,1:T(8,128)(2,1)S(1)}, u32[]{:S(2)}, u32[]{:S(2)}) %collective-permute-start) | collective-permute-done | bytes 1048608 | tf_op jit(solution)/shard_map/ppermute | solution.py:14
  38.7 12.4 %collective-permute-done.1 = bf16[128,32,128]{0,2,1:T(8,128)(2,1)} collective-permute-done((bf16[128,32,128]{0,2,1:T(8,128)(2,1)S(1)}, bf16[128,32,128]{0,2,1:T(8,128)(2,1)}, u32[]{:S(2)}, u32[]{:S(2)}) %collective-permute-start.1) | collective-permute-done | bytes 1048608 | tf_op jit(solution)/shard_map/ppermute | solution.py:14
  51.1 2.4 pad_maximum_fusion
  53.5 2.9 %copy.27 = bf16[384,32,128]{2,0,1:T(8,128)(2,1)} copy(bf16[384,32,128]{0,2,1:T(8,128)(2,1)S(1)} %pad_maximum_fusion) | data formatting | bytes 6291456 | tf_op jit(solution)/shard_map/while | solution.py:82
  56.4 8.4 %all-gather.3.cloned.1.call-done = bf16[512,32,128]{2,1,0:T(8,128)(2,1)} async-done(((bf16[128,32,128]{2,1,0:T(8,128)(2,1)}), bf16[512,32,128]{2,1,0:T(8,128)(2,1)}) %all-gather.3.cloned.1.call-update) | async-done | bytes 4194320 | tf_op jit(solution)/shard_map/all_gather | solution.py:152
  64.8 5.8 %copy.26 = bf16[2,256,32,128]{3,1,2,0:T(8,128)(2,1)} copy(bf16[2,256,32,128]{3,2,1,0:T(8,128)(2,1)} %bitcast.45) | data formatting | bytes 8388608 | tf_op jit(solution)/shard_map/while | solution.py:82
  70.7 50.3 %all-gather.5.cloned.1.call-done = bf16[512,32,128]{2,1,0:T(8,128)(2,1)} async-done(((bf16[128,32,128]{2,1,0:T(8,128)(2,1)}), bf16[512,32,128]{2,1,0:T(8,128)(2,1)}) %all-gather.5.cloned.1.call-update) | async-done | bytes 4194320 | tf_op jit(solution)/shard_map/all_gather | solution.py:155
  121.0 6.0 %copy.28 = bf16[2,256,32,128]{3,1,2,0:T(8,128)(2,1)} copy(bf16[2,256,32,128]{3,2,1,0:T(8,128)(2,1)} %bitcast.46) | data formatting | bytes 8388608 | tf_op jit(solution)/shard_map/while | solution.py:82
  127.0 3.4 %broadcast_in_dim.61 = f32[384,32,128]{2,0,1:T(8,128)} broadcast(f32[]{:T(128)} %constant.59.clone.1), dimensions={} | broadcast | bytes 6291460 | tf_op jit(solution)/shard_map/broadcast_in_dim | solution.py:26
  130.4 41.3 %while.14 = (s32[]{:T(128)}, f32[384,32]{0,1:T(8,128)S(1)}, f32[384,32]{0,1:T(8,128)S(1)}, f32[384,32,128]{2,0,1:T(8,128)}, s32[384]{0:T(512)S(1)}, /*index=5*/s...) while((s32[]{:T(128)}, f32[384,32]{0,1:T(8,128)S(1)}, ...), condition=%wide.region_9.10_spmd, body=%wide.region_3.9_spmd.sunk | while | flops 1674141696 | bytes 104477920 | solution.py:82
  131.9 19.2 %conditional.2 = ((f32[384,32]{0,1:T(8,128)S(1)}, f32[384,32]{0,1:T(8,128)S(1)}, f32[384,32,128]{2,0,1:T(8,128)})) conditional(s32[]{:T(128)} %convert_element_type.41, (f32[384,32]{0,1:T(8,128)S(1)}, f32[384,32]{0,1:T(8,128)S(1)}, f32[384,32,128]{2,0,1:T(8,128)}) %tuple.50, (pred[384,256]{0,1:T(8,128)(4,1)S(1)}, bf16[2,256,32,128]{3,1,2,0:T(8,128)(2,1)}, ...), branch_computations={%region_5.5_spmd, %region_6.8_spmd} | conditional | flops 1673748480 | bytes 104370152 | solution.py:59
  132.0 4.5 %fusion.3 = (f32[384,32]{0,1:T(8,128)S(1)}, f32[32,256,384]{2,1,0:T(8,128)S(1)}) fusion(f32[384,256]{0,1:T(8,128)S(1)} %subtract_convert_fusion, f32[32]{0:T(128)S(1)} %get-tuple-element.141, pred[384,256]{0,1:T(8,128)(4,1)S(1)} %get-tuple-element.137, bf16[384,32,128]{2,0,1:T(8,128)(2,1)S(1)} %get-tuple-element.140, ...), kind=kOutput, calls=%fused_computation.5 | convolution fusion | flops 821022720 | bytes 18367104 | tf_op jit(solution)/shard_map/while/body/eval_jaxpr/cond/branch_1_fun/qhd,khd->qhk/dot_general | solution.py:36
  136.6 4.3 %fusion.2 = f32[384,32]{0,1:T(8,128)S(1)} fusion(f32[32,256,384]{2,1,0:T(8,128)S(1)} %get-tuple-element.239, f32[384,32]{0,1:T(8,128)S(1)} %max.8, f32[384,256]{0,1:T(8,128)S(1)} %subtract_convert_fusion, f32[32]{0:T(128)S(1)} %get-tuple-element.141, pred[384,256]{0,1:T(8,128)(4,1)S(1)} %get-tuple-element.137), kind=kLoop, calls=%fused_computation.4 | loop fusion | flops 22007808 | bytes 13172864 | tf_op jit(solution)/shard_map/while/body/eval_jaxpr/cond/branch_1_fun/reduce_sum | solution.py:46
  140.9 7.5 %bitcast_add_fusion = f32[384,32,128]{2,0,1:T(8,128)S(1)} fusion(f32[384,32,128]{2,0,1:T(8,128)S(1)} %bitcast.44, f32[384,32]{0,1:T(8,128)S(1)} %get-tuple-element.230, f32[32,256,384]{2,1,0:T(8,128)S(1)} %get-tuple-element.239, f32[384,32]{0,1:T(8,128)S(1)} %max.8, f32[384,256]{0,1:T(8,128)S(1)} %subtract_convert_fusion, f32[32]{0:T(128)S(1)} %get-tuple-element.141, ...), kind=kOutput, calls=%fused_computation.6 | convolution fusion | flops 830472192 | bytes 27853440 | tf_op jit(solution)/shard_map/while/body/eval_jaxpr/cond/branch_1_fun/qhk,khd->qhd/dot_general | solution.py:47
  148.4 2.7 copy-done
  152.5 19.2 %conditional.2 = ((f32[384,32]{0,1:T(8,128)S(1)}, f32[384,32]{0,1:T(8,128)S(1)}, f32[384,32,128]{2,0,1:T(8,128)})) conditional(s32[]{:T(128)} %convert_element_type.41, (f32[384,32]{0,1:T(8,128)S(1)}, f32[384,32]{0,1:T(8,128)S(1)}, f32[384,32,128]{2,0,1:T(8,128)}) %tuple.50, (pred[384,256]{0,1:T(8,128)(4,1)S(1)}, bf16[2,256,32,128]{3,1,2,0:T(8,128)(2,1)}, ...), branch_computations={%region_5.5_spmd, %region_6.8_spmd} | conditional | flops 1673748480 | bytes 104370152 | solution.py:59
  152.7 4.5 %fusion.3 = (f32[384,32]{0,1:T(8,128)S(1)}, f32[32,256,384]{2,1,0:T(8,128)S(1)}) fusion(f32[384,256]{0,1:T(8,128)S(1)} %subtract_convert_fusion, f32[32]{0:T(128)S(1)} %get-tuple-element.141, pred[384,256]{0,1:T(8,128)(4,1)S(1)} %get-tuple-element.137, bf16[384,32,128]{2,0,1:T(8,128)(2,1)S(1)} %get-tuple-element.140, ...), kind=kOutput, calls=%fused_computation.5 | convolution fusion | flops 821022720 | bytes 18367104 | tf_op jit(solution)/shard_map/while/body/eval_jaxpr/cond/branch_1_fun/qhd,khd->qhk/dot_general | solution.py:36
  157.2 4.3 %fusion.2 = f32[384,32]{0,1:T(8,128)S(1)} fusion(f32[32,256,384]{2,1,0:T(8,128)S(1)} %get-tuple-element.239, f32[384,32]{0,1:T(8,128)S(1)} %max.8, f32[384,256]{0,1:T(8,128)S(1)} %subtract_convert_fusion, f32[32]{0:T(128)S(1)} %get-tuple-element.141, pred[384,256]{0,1:T(8,128)(4,1)S(1)} %get-tuple-element.137), kind=kLoop, calls=%fused_computation.4 | loop fusion | flops 22007808 | bytes 13172864 | tf_op jit(solution)/shard_map/while/body/eval_jaxpr/cond/branch_1_fun/reduce_sum | solution.py:46
  161.6 7.5 %bitcast_add_fusion = f32[384,32,128]{2,0,1:T(8,128)S(1)} fusion(f32[384,32,128]{2,0,1:T(8,128)S(1)} %bitcast.44, f32[384,32]{0,1:T(8,128)S(1)} %get-tuple-element.230, f32[32,256,384]{2,1,0:T(8,128)S(1)} %get-tuple-element.239, f32[384,32]{0,1:T(8,128)S(1)} %max.8, f32[384,256]{0,1:T(8,128)S(1)} %subtract_convert_fusion, f32[32]{0:T(128)S(1)} %get-tuple-element.141, ...), kind=kOutput, calls=%fused_computation.6 | convolution fusion | flops 830472192 | bytes 27853440 | tf_op jit(solution)/shard_map/while/body/eval_jaxpr/cond/branch_1_fun/qhk,khd->qhd/dot_general | solution.py:47
  169.1 2.7 copy-done
  171.7 2.5 fusion.25
  176.1 3.4 %collective-permute-start.7 = (f32[128,32,128]{2,0,1:T(8,128)S(1)}, f32[128,32,128]{2,0,1:T(8,128)S(1)}, u32[]{:S(2)}, u32[]{:S(2)}) collective-permute-start(f32[128,32,128]{2,0,1:T(8,128)S(1)} %get-tuple-element.243), channel_id=1, source_target_pairs={{0,8},{4,12},{8,16},{12,20},{16,24},{20,28},{24,32},{28,36},{32,40... | collective-permute-start | bytes 6291464 | tf_op jit(solution)/shard_map/ppermute | solution.py:14
  179.6 3.2 %collective-permute-start.2 = (f32[128,32]{0,1:T(8,128)S(1)}, f32[128,32]{0,1:T(8,128)S(1)}, u32[]{:S(2)}, u32[]{:S(2)}) collective-permute-start(f32[128,32]{0,1:T(8,128)S(1)} %get-tuple-element.246), channel_id=1, source_target_pairs={{0,4},{4,8},{8,12},{12,16},{16,20},{20,24},{24,28},{28,32},{32,36}... | collective-permute-start | bytes 49160 | tf_op jit(solution)/shard_map/ppermute | solution.py:14
  182.8 2.2 collective-permute-start.3
  185.0 3.4 %collective-permute-start.5 = (f32[128,32]{0,1:T(8,128)S(1)}, f32[128,32]{0,1:T(8,128)S(1)}, u32[]{:S(2)}, u32[]{:S(2)}) collective-permute-start(f32[128,32]{0,1:T(8,128)S(1)} %get-tuple-element.247), channel_id=1, source_target_pairs={{0,8},{4,12},{8,16},{12,20},{16,24},{20,28},{24,32},{28,36},{32,40... | collective-permute-start | bytes 49160 | tf_op jit(solution)/shard_map/ppermute | solution.py:14
  188.4 61.8 %collective-permute-done.2 = f32[128,32]{0,1:T(8,128)S(1)} collective-permute-done((f32[128,32]{0,1:T(8,128)S(1)}, f32[128,32]{0,1:T(8,128)S(1)}, u32[]{:S(2)}, u32[]{:S(2)}) %collective-permute-start.2) | collective-permute-done | bytes 16416 | tf_op jit(solution)/shard_map/ppermute | solution.py:14
  252.1 7.0 %collective-permute-done.6 = f32[128,32]{0,1:T(8,128)S(1)} collective-permute-done((f32[128,32]{0,1:T(8,128)S(1)}, f32[128,32]{0,1:T(8,128)S(1)}, u32[]{:S(2)}, u32[]{:S(2)}) %collective-permute-start.6) | collective-permute-done | bytes 16416 | tf_op jit(solution)/shard_map/ppermute | solution.py:14
  259.2 7.0 %copy_bitcast_fusion = bf16[128,4096]{1,0:T(8,128)(2,1)} fusion(f32[128,32]{0,1:T(8,128)S(1)} %get-tuple-element.233, f32[128,32,128]{2,0,1:T(8,128)S(1)} %collective-permute-done.7, f32[128,32]{0,1:T(8,128)S(1)} %get-tuple-element.237, f32[128,32]{0,1:T(8,128)S(1)} %get-tuple-element.236, f32[128,32,128]{2,0,1:T(8,128)S(1)} %collective-permute-done.4, ...), kind=kLoop, calls=%fused_computation.27 | loop fusion | flops 4194304 | bytes 7421952 | tf_op jit(solution)/shard_map/reshape | solution.py:164
  (63 shorter events, 8.5 us)
Async XLA Ops:
  6.5 5.1 %copy-start.3 = (bf16[128,4096]{1,0:T(8,128)(2,1)S(1)}, bf16[128,4096]{1,0:T(8,128)(2,1)}, u32[]{:S(2)}) copy-start(bf16[128,4096]{1,0:T(8,128)(2,1)} %param.9) | copy-start | bytes 3145732
  6.5 12.9 %copy-start.6 = (s32[128]{0:T(128)S(1)}, s32[128]{0:T(128)}, u32[]{:S(2)}) copy-start(s32[128]{0:T(128)} %param.12) | copy-start | bytes 1540
  6.5 58.3 %all-gather.3.cloned.1.call-start = ((), (), s32[]{:S(2)}) async-start(), calls=%async_computation | async-start | bytes 5242880 | tf_op jit(solution)/shard_map/all_gather | solution.py:152
  9.1 111.9 %all-gather.5.cloned.1.call-start = ((), (), s32[]{:S(2)}) async-start(), calls=%async_computation.1 | async-start | bytes 5242880 | tf_op jit(solution)/shard_map/all_gather | solution.py:155
  12.3 25.4 %copy-start.1 = (bf16[128,4096]{0,1:T(8,128)(2,1)}, bf16[128,4096]{0,1:T(8,128)(2,1)S(1)}, u32[]{:S(2)}) copy-start(bf16[128,4096]{0,1:T(8,128)(2,1)S(1)} %copy.25) | copy-start | bytes 3145732
  12.3 25.4 %collective-permute-start = (bf16[128,32,128]{0,2,1:T(8,128)(2,1)S(1)}, bf16[128,32,128]{0,2,1:T(8,128)(2,1)S(1)}, u32[]{:S(2)}, u32[]{:S(2)}) collective-permute-start(bf16[128,32,128]{0,2,1:T(8,128)(2,1)S(1)} %bitcast.49), channel_id=1, source_target_pairs={{4,0},{8,4},{12,8},{16,12},{20,16},{24,20},{28,24},{32,28},{36,32}... | collective-permute-start | bytes 3145736 | tf_op jit(solution)/shard_map/ppermute | solution.py:14
  16.2 34.9 %collective-permute-start.1 = (bf16[128,32,128]{0,2,1:T(8,128)(2,1)S(1)}, bf16[128,32,128]{0,2,1:T(8,128)(2,1)}, u32[]{:S(2)}, u32[]{:S(2)}) collective-permute-start(bf16[128,32,128]{0,2,1:T(8,128)(2,1)S(1)} %bitcast.50), channel_id=1, source_target_pairs={{8,0},{12,4},{16,8},{20,12},{24,16},{28,20},{32,24},{36,28},{40,32... | collective-permute-start | bytes 3145736 | tf_op jit(solution)/shard_map/ppermute | solution.py:14
  37.6 1.0 copy-start.4
  121.0 9.4 %copy-start.2 = (bf16[384,32,128]{2,0,1:T(8,128)(2,1)S(1)}, bf16[384,32,128]{2,0,1:T(8,128)(2,1)}, u32[]{:S(2)}) copy-start(bf16[384,32,128]{2,0,1:T(8,128)(2,1)} %copy.27) | copy-start | bytes 9437188
  121.0 9.4 %copy-start.5 = (f32[32]{0:T(128)S(1)}, f32[32]{0:T(128)}, u32[]{:S(2)}) copy-start(f32[32]{0:T(128)} %param.13) | copy-start | bytes 388
  131.9 9.0 %slice-start = ((s8[6291456]{0:T(1024)(128)(4,1)}), s8[4194304]{0:T(1024)(128)(4,1)S(1)}, s32[]{:S(2)}) async-start(s8[6291456]{0:T(1024)(128)(4,1)} %bitcast.43), calls=%async_computation.2 | async-start | bytes 8388608 | tf_op jit(solution)/shard_map/while/body/eval_jaxpr/cond
  132.0 8.9 %slice-start.1 = ((s8[6291456]{0:T(1024)(128)(4,1)}), s8[2097152]{0:T(1024)(128)(4,1)S(1)}, s32[]{:S(2)}) async-start(s8[6291456]{0:T(1024)(128)(4,1)} %bitcast.43), calls=%async_computation.3 | async-start | bytes 4194304 | tf_op jit(solution)/shard_map/while/body/eval_jaxpr/cond
  148.4 2.7 copy-start
  152.5 9.0 %slice-start = ((s8[6291456]{0:T(1024)(128)(4,1)}), s8[4194304]{0:T(1024)(128)(4,1)S(1)}, s32[]{:S(2)}) async-start(s8[6291456]{0:T(1024)(128)(4,1)} %bitcast.43), calls=%async_computation.2 | async-start | bytes 8388608 | tf_op jit(solution)/shard_map/while/body/eval_jaxpr/cond
  152.7 8.9 %slice-start.1 = ((s8[6291456]{0:T(1024)(128)(4,1)}), s8[2097152]{0:T(1024)(128)(4,1)S(1)}, s32[]{:S(2)}) async-start(s8[6291456]{0:T(1024)(128)(4,1)} %bitcast.43), calls=%async_computation.3 | async-start | bytes 4194304 | tf_op jit(solution)/shard_map/while/body/eval_jaxpr/cond
  169.0 2.7 copy-start
  174.2 84.9 %collective-permute-start.4 = (f32[128,32,128]{2,0,1:T(8,128)S(1)}, f32[128,32,128]{2,0,1:T(8,128)S(1)}, u32[]{:S(2)}, u32[]{:S(2)}) collective-permute-start(f32[128,32,128]{2,0,1:T(8,128)S(1)} %get-tuple-element.242), channel_id=1, source_target_pairs={{0,4},{4,8},{8,12},{12,16},{16,20},{20,24},{24,28},{28,32},{32,36}... | collective-permute-start | bytes 6291464 | tf_op jit(solution)/shard_map/ppermute | solution.py:14
  176.1 83.0 %collective-permute-start.7 = (f32[128,32,128]{2,0,1:T(8,128)S(1)}, f32[128,32,128]{2,0,1:T(8,128)S(1)}, u32[]{:S(2)}, u32[]{:S(2)}) collective-permute-start(f32[128,32,128]{2,0,1:T(8,128)S(1)} %get-tuple-element.243), channel_id=1, source_target_pairs={{0,8},{4,12},{8,16},{12,20},{16,24},{20,28},{24,32},{28,36},{32,40... | collective-permute-start | bytes 6291464 | tf_op jit(solution)/shard_map/ppermute | solution.py:14
  179.6 70.6 %collective-permute-start.2 = (f32[128,32]{0,1:T(8,128)S(1)}, f32[128,32]{0,1:T(8,128)S(1)}, u32[]{:S(2)}, u32[]{:S(2)}) collective-permute-start(f32[128,32]{0,1:T(8,128)S(1)} %get-tuple-element.246), channel_id=1, source_target_pairs={{0,4},{4,8},{8,12},{12,16},{16,20},{20,24},{24,28},{28,32},{32,36}... | collective-permute-start | bytes 49160 | tf_op jit(solution)/shard_map/ppermute | solution.py:14
  182.8 69.3 %collective-permute-start.3 = (f32[128,32]{0,1:T(8,128)S(1)}, f32[128,32]{0,1:T(8,128)S(1)}, u32[]{:S(2)}, u32[]{:S(2)}) collective-permute-start(f32[128,32]{0,1:T(8,128)S(1)} %get-tuple-element.245), channel_id=1, source_target_pairs={{0,4},{4,8},{8,12},{12,16},{16,20},{20,24},{24,28},{28,32},{32,36}... | collective-permute-start | bytes 49160 | tf_op jit(solution)/shard_map/ppermute | solution.py:14
  185.0 67.1 %collective-permute-start.5 = (f32[128,32]{0,1:T(8,128)S(1)}, f32[128,32]{0,1:T(8,128)S(1)}, u32[]{:S(2)}, u32[]{:S(2)}) collective-permute-start(f32[128,32]{0,1:T(8,128)S(1)} %get-tuple-element.247), channel_id=1, source_target_pairs={{0,8},{4,12},{8,16},{12,20},{16,24},{20,28},{24,32},{28,36},{32,40... | collective-permute-start | bytes 49160 | tf_op jit(solution)/shard_map/ppermute | solution.py:14
  250.2 8.9 %collective-permute-start.6 = (f32[128,32]{0,1:T(8,128)S(1)}, f32[128,32]{0,1:T(8,128)S(1)}, u32[]{:S(2)}, u32[]{:S(2)}) collective-permute-start(f32[128,32]{0,1:T(8,128)S(1)} %get-tuple-element.244), channel_id=1, source_target_pairs={{0,8},{4,12},{8,16},{12,20},{16,24},{20,28},{24,32},{28,36},{32,40... | collective-permute-start | bytes 49160 | tf_op jit(solution)/shard_map/ppermute | solution.py:14
Sparse Core Ops, SparseCore 0:
  9.5 55.3 all-gather.2
  66.9 53.9 all-gather.4
where the time goes:
time: 274 us; the launch traced here: 273 us
  waiting for transfers between devices  157 us (57%)
  local copies, waits for them, and re-layouts  32.9 us (12%)
  matrix products  24 us (9%)
  starting transfers between devices  23.2 us (8%)
  other arithmetic  20.6 us (8%)
  between operations  13.6 us (5%)
    ppermute x8, waiting for transfers between devices, shifted(): lax.ppermute(value, axis, [(source, source + steps) for source in range(f...  98.4 us
    all_gather x1, waiting for transfers between devices, per_device(): lax.all_gather(value_states.reshape(rows_dev, head_count, head_width), 'i...  50.3 us
    ppermute x8, starting transfers between devices, shifted(): lax.ppermute(value, axis, [(source, source + steps) for source in range(f...  23.2 us
    dot_general x2, matrix products, update(): jnp.einsum('qhk,khd->qhd', weights.astype(jnp.bfloat16), value_slab, pref...  15 us
    while x3, local copies, waits for them, and re-layouts, attend_keys(): result, unused = lax.scan(scan_step, status, stacked)  14.8 us
    dot_general x2, matrix products, update(): jnp.einsum('qhd,khd->qhk', query_rows, key_slab, preferred_element_type=j...  9.01 us
    reduce_sum x2, other arithmetic, update(): row_total = row_total * rescale + jnp.sum(weights, axis=-1)  8.57 us
    all_gather x1, waiting for transfers between devices, per_device(): lax.all_gather(key_states.reshape(rows_dev, head_count, head_width), 'inn...  8.4 us
  transfers between devices with their start and end apart: 10, of which 6 were waited for; matrix products, arithmetic and copies ran while one was open for 6% of the time, Pallas kernels for 0%

commit v1 on v0

--- a/solution.py
+++ b/solution.py
@@ -136,6 +136,13 @@
 
 
 def per_device(query_states, key_states, value_states, doc_lengths, slopes):
+
+    def things_trace(arr_in, axis_id):
+        all_rows = lax.axis_size(axis_id)
+        y = jnp.stack(all_rows * [arr_in])
+        inter = lax.all_to_all(y, axis_id, 0, 0)
+        return jnp.concatenate(inter, axis=0)
+
     rows_dev = query_states.shape[0]
     head_count = slopes.shape[0]
     head_width = query_states.shape[1] // head_count
@@ -152,9 +159,7 @@
         lax.all_gather(
             key_states.reshape(rows_dev, head_count, head_width), "inner", axis=0, tiled=True
         ),
-        lax.all_gather(
-            value_states.reshape(rows_dev, head_count, head_width), "inner", axis=0, tiled=True
-        ),
+        things_trace(value_states.reshape(rows_dev, head_count, head_width), "inner"),
     )
     key_pos = group_start + jnp.arange(portions[0].shape[0], dtype=jnp.int32)
     status = attend_keys(

time: 274 us -> 260 us (0.949)
  waiting for transfers between devices: 157 us -> 136 us
  starting transfers between devices: 23.2 us -> 28.5 us
    all_gather x1 -> x0, waiting for transfers between devices: 50.3 us -> none  [per_device(): lax.all_gather(value_states.reshape(rows_dev, head_count, head_width), 'i...]
    all_to_all x0 -> x1, waiting for transfers between devices: none -> 37.9 us  [things_trace(): inter = lax.all_to_all(y, axis_id, 0, 0)]
    all_gather x1, waiting for transfers between devices: 8.4 us -> 0.01 us  [per_device(): lax.all_gather(key_states.reshape(rows_dev, head_count, head_width), 'inn...]
    all_to_all x0 -> x1, starting transfers between devices: none -> 4.97 us  [things_trace(): inter = lax.all_to_all(y, axis_id, 0, 0)]
  transfers between devices with their start and end apart: 10 -> 10, of which waited for: 6 -> 5; matrix products, arithmetic and copies ran while one was open for 6% -> 7% of each run, Pallas kernels for 0% -> 0%
where the time goes in v1:
time: 260 us; the launch traced here: 259 us
  waiting for transfers between devices  136 us (52%)
  local copies, waits for them, and re-layouts  34.5 us (13%)
  starting transfers between devices  28.5 us (11%)
  matrix products  24 us (9%)
  other arithmetic  20.5 us (8%)
  between operations  13.6 us (5%)
    ppermute x8, waiting for transfers between devices, shifted(): lax.ppermute(value, axis, [(source, source + steps) for source in range(f...  98.2 us
    all_to_all x1, waiting for transfers between devices, things_trace(): inter = lax.all_to_all(y, axis_id, 0, 0)  37.9 us
    ppermute x8, starting transfers between devices, shifted(): lax.ppermute(value, axis, [(source, source + steps) for source in range(f...  23.5 us
    dot_general x2, matrix products, update(): jnp.einsum('qhk,khd->qhd', weights.astype(jnp.bfloat16), value_slab, pref...  15 us
    while x3, local copies, waits for them, and re-layouts, attend_keys(): result, unused = lax.scan(scan_step, status, stacked)  14.9 us
    dot_general x2, matrix products, update(): jnp.einsum('qhd,khd->qhk', query_rows, key_slab, preferred_element_type=j...  9.02 us
    reduce_sum x2, other arithmetic, update(): row_total = row_total * rescale + jnp.sum(weights, axis=-1)  8.57 us
    reshape x1, other arithmetic, per_device(): return normalize(combined).reshape(rows_dev, head_count * head_width)  6.98 us
  transfers between devices with their start and end apart: 10, of which 5 were waited for; matrix products, arithmetic and copies ran while one was open for 7% of the time, Pallas kernels for 0%

profile of v1, /device:TPU:256, one launch (start us, length us, event | category | flops | bytes accessed | tf_op | source)
XLA Modules:
  0.0 258.8 jit_solution(17096342022326641731)
XLA Ops:
  6.5 2.4 copy.32
  10.5 2.6 %stack.3 = bf16[4,128,32,128]{3,2,1,0:T(8,128)(2,1)} broadcast(bf16[128,32,128]{2,1,0:T(8,128)(2,1)S(1)} %bitcast.45), dimensions={1,2,3} | broadcast | bytes 5242880 | tf_op jit(solution)/shard_map/stack | solution.py:142
  13.1 5.0 %all-to-all-start = ((bf16[4,128,32,128]{3,2,1,0:T(8,128)(2,1)}), bf16[4,128,32,128]{3,2,1,0:T(8,128)(2,1)}, u32[]{:S(2)}, u32[]{:S(2)}) async-start(bf16[4,128,32,128]{3,2,1,0:T(8,128)(2,1)} %stack.3), calls=%async_computation | async-start | bytes 8388608 | tf_op jit(solution)/shard_map/all_to_all | solution.py:143
  18.8 3.9 %collective-permute-start = (bf16[128,32,128]{0,2,1:T(8,128)(2,1)S(1)}, bf16[128,32,128]{0,2,1:T(8,128)(2,1)S(1)}, u32[]{:S(2)}, u32[]{:S(2)}) collective-permute-start(bf16[128,32,128]{0,2,1:T(8,128)(2,1)S(1)} %bitcast.48), channel_id=1, source_target_pairs={{4,0},{8,4},{12,8},{16,12},{20,16},{24,20},{28,24},{32,28},{36,32}... | collective-permute-start | bytes 3145736 | tf_op jit(solution)/shard_map/ppermute | solution.py:14
  22.7 3.3 %collective-permute-start.1 = (bf16[128,32,128]{0,2,1:T(8,128)(2,1)S(1)}, bf16[128,32,128]{0,2,1:T(8,128)(2,1)}, u32[]{:S(2)}, u32[]{:S(2)}) collective-permute-start(bf16[128,32,128]{0,2,1:T(8,128)(2,1)S(1)} %bitcast.49), channel_id=1, source_target_pairs={{8,0},{12,4},{16,8},{20,12},{24,16},{28,20},{32,24},{36,28},{40,32... | collective-permute-start | bytes 3145736 | tf_op jit(solution)/shard_map/ppermute | solution.py:14
  26.9 17.2 %collective-permute-done = bf16[128,32,128]{0,2,1:T(8,128)(2,1)S(1)} collective-permute-done((bf16[128,32,128]{0,2,1:T(8,128)(2,1)S(1)}, bf16[128,32,128]{0,2,1:T(8,128)(2,1)S(1)}, u32[]{:S(2)}, u32[]{:S(2)}) %collective-permute-start) | collective-permute-done | bytes 1048608 | tf_op jit(solution)/shard_map/ppermute | solution.py:14
  45.1 12.5 %collective-permute-done.1 = bf16[128,32,128]{0,2,1:T(8,128)(2,1)} collective-permute-done((bf16[128,32,128]{0,2,1:T(8,128)(2,1)S(1)}, bf16[128,32,128]{0,2,1:T(8,128)(2,1)}, u32[]{:S(2)}, u32[]{:S(2)}) %collective-permute-start.1) | collective-permute-done | bytes 1048608 | tf_op jit(solution)/shard_map/ppermute | solution.py:14
  57.6 2.3 pad_maximum_fusion
  59.9 3.1 %copy.27 = bf16[384,32,128]{2,0,1:T(8,128)(2,1)} copy(bf16[384,32,128]{0,2,1:T(8,128)(2,1)S(1)} %pad_maximum_fusion) | data formatting | bytes 6291456 | tf_op jit(solution)/shard_map/while | solution.py:82
  63.0 37.9 %all-to-all-done = bf16[4,128,32,128]{3,2,1,0:T(8,128)(2,1)} async-done(((bf16[4,128,32,128]{3,2,1,0:T(8,128)(2,1)}), bf16[4,128,32,128]{3,2,1,0:T(8,128)(2,1)}, u32[]{:S(2)}, u32[]{:S(2)}) %all-to-all-start) | async-done | bytes 4194336 | tf_op jit(solution)/shard_map/all_to_all | solution.py:143
  100.9 5.8 %copy.28 = bf16[2,256,32,128]{3,1,2,0:T(8,128)(2,1)} copy(bf16[2,256,32,128]{3,2,1,0:T(8,128)(2,1)} %bitcast.9) | data formatting | bytes 8388608 | tf_op jit(solution)/shard_map/while | solution.py:82
  106.8 6.0 %copy.26 = bf16[2,256,32,128]{3,1,2,0:T(8,128)(2,1)} copy(bf16[2,256,32,128]{3,2,1,0:T(8,128)(2,1)} %bitcast.46) | data formatting | bytes 8388608 | tf_op jit(solution)/shard_map/while | solution.py:82
  112.8 3.4 %broadcast_in_dim.61 = f32[384,32,128]{2,0,1:T(8,128)} broadcast(f32[]{:T(128)} %constant.59.clone.1), dimensions={} | broadcast | bytes 6291460 | tf_op jit(solution)/shard_map/broadcast_in_dim | solution.py:26
  116.2 41.3 %while.14 = (s32[]{:T(128)}, f32[384,32]{0,1:T(8,128)S(1)}, f32[384,32]{0,1:T(8,128)S(1)}, f32[384,32,128]{2,0,1:T(8,128)}, s32[384]{0:T(512)S(1)}, /*index=5*/s...) while((s32[]{:T(128)}, f32[384,32]{0,1:T(8,128)S(1)}, ...), condition=%wide.region_9.10_spmd, body=%wide.region_3.9_spmd.sunk | while | flops 1674141696 | bytes 104477920 | solution.py:82
  117.7 19.2 %conditional.2 = ((f32[384,32]{0,1:T(8,128)S(1)}, f32[384,32]{0,1:T(8,128)S(1)}, f32[384,32,128]{2,0,1:T(8,128)})) conditional(s32[]{:T(128)} %convert_element_type.41, (f32[384,32]{0,1:T(8,128)S(1)}, f32[384,32]{0,1:T(8,128)S(1)}, f32[384,32,128]{2,0,1:T(8,128)}) %tuple.50, (pred[384,256]{0,1:T(8,128)(4,1)S(1)}, bf16[2,256,32,128]{3,1,2,0:T(8,128)(2,1)}, ...), branch_computations={%region_5.5_spmd, %region_6.8_spmd} | conditional | flops 1673748480 | bytes 104370152 | solution.py:59
  117.8 4.5 %fusion.3 = (f32[384,32]{0,1:T(8,128)S(1)}, f32[32,256,384]{2,1,0:T(8,128)S(1)}) fusion(f32[384,256]{0,1:T(8,128)S(1)} %subtract_convert_fusion, f32[32]{0:T(128)S(1)} %get-tuple-element.141, pred[384,256]{0,1:T(8,128)(4,1)S(1)} %get-tuple-element.137, bf16[384,32,128]{2,0,1:T(8,128)(2,1)S(1)} %get-tuple-element.140, ...), kind=kOutput, calls=%fused_computation.5 | convolution fusion | flops 821022720 | bytes 18367104 | tf_op jit(solution)/shard_map/while/body/eval_jaxpr/cond/branch_1_fun/qhd,khd->qhk/dot_general | solution.py:36
  122.4 4.3 %fusion.2 = f32[384,32]{0,1:T(8,128)S(1)} fusion(f32[32,256,384]{2,1,0:T(8,128)S(1)} %get-tuple-element.239, f32[384,32]{0,1:T(8,128)S(1)} %max.8, f32[384,256]{0,1:T(8,128)S(1)} %subtract_convert_fusion, f32[32]{0:T(128)S(1)} %get-tuple-element.141, pred[384,256]{0,1:T(8,128)(4,1)S(1)} %get-tuple-element.137), kind=kLoop, calls=%fused_computation.4 | loop fusion | flops 22007808 | bytes 13172864 | tf_op jit(solution)/shard_map/while/body/eval_jaxpr/cond/branch_1_fun/reduce_sum | solution.py:46
  126.7 7.5 %bitcast_add_fusion = f32[384,32,128]{2,0,1:T(8,128)S(1)} fusion(f32[384,32,128]{2,0,1:T(8,128)S(1)} %bitcast.44, f32[384,32]{0,1:T(8,128)S(1)} %get-tuple-element.230, f32[32,256,384]{2,1,0:T(8,128)S(1)} %get-tuple-element.239, f32[384,32]{0,1:T(8,128)S(1)} %max.8, f32[384,256]{0,1:T(8,128)S(1)} %subtract_convert_fusion, f32[32]{0:T(128)S(1)} %get-tuple-element.141, ...), kind=kOutput, calls=%fused_computation.6 | convolution fusion | flops 830472192 | bytes 27853440 | tf_op jit(solution)/shard_map/while/body/eval_jaxpr/cond/branch_1_fun/qhk,khd->qhd/dot_general | solution.py:47
  134.2 2.7 %copy-done = f32[384,32,128]{2,0,1:T(8,128)} copy-done((f32[384,32,128]{2,0,1:T(8,128)}, f32[384,32,128]{2,0,1:T(8,128)S(1)}, u32[]{:S(2)}) %copy-start) | copy-done | bytes 6291480 | tf_op jit(solution)/shard_map/while/body/eval_jaxpr/cond
  138.3 19.2 %conditional.2 = ((f32[384,32]{0,1:T(8,128)S(1)}, f32[384,32]{0,1:T(8,128)S(1)}, f32[384,32,128]{2,0,1:T(8,128)})) conditional(s32[]{:T(128)} %convert_element_type.41, (f32[384,32]{0,1:T(8,128)S(1)}, f32[384,32]{0,1:T(8,128)S(1)}, f32[384,32,128]{2,0,1:T(8,128)}) %tuple.50, (pred[384,256]{0,1:T(8,128)(4,1)S(1)}, bf16[2,256,32,128]{3,1,2,0:T(8,128)(2,1)}, ...), branch_computations={%region_5.5_spmd, %region_6.8_spmd} | conditional | flops 1673748480 | bytes 104370152 | solution.py:59
  138.5 4.5 %fusion.3 = (f32[384,32]{0,1:T(8,128)S(1)}, f32[32,256,384]{2,1,0:T(8,128)S(1)}) fusion(f32[384,256]{0,1:T(8,128)S(1)} %subtract_convert_fusion, f32[32]{0:T(128)S(1)} %get-tuple-element.141, pred[384,256]{0,1:T(8,128)(4,1)S(1)} %get-tuple-element.137, bf16[384,32,128]{2,0,1:T(8,128)(2,1)S(1)} %get-tuple-element.140, ...), kind=kOutput, calls=%fused_computation.5 | convolution fusion | flops 821022720 | bytes 18367104 | tf_op jit(solution)/shard_map/while/body/eval_jaxpr/cond/branch_1_fun/qhd,khd->qhk/dot_general | solution.py:36
  143.0 4.3 %fusion.2 = f32[384,32]{0,1:T(8,128)S(1)} fusion(f32[32,256,384]{2,1,0:T(8,128)S(1)} %get-tuple-element.239, f32[384,32]{0,1:T(8,128)S(1)} %max.8, f32[384,256]{0,1:T(8,128)S(1)} %subtract_convert_fusion, f32[32]{0:T(128)S(1)} %get-tuple-element.141, pred[384,256]{0,1:T(8,128)(4,1)S(1)} %get-tuple-element.137), kind=kLoop, calls=%fused_computation.4 | loop fusion | flops 22007808 | bytes 13172864 | tf_op jit(solution)/shard_map/while/body/eval_jaxpr/cond/branch_1_fun/reduce_sum | solution.py:46
  147.4 7.5 %bitcast_add_fusion = f32[384,32,128]{2,0,1:T(8,128)S(1)} fusion(f32[384,32,128]{2,0,1:T(8,128)S(1)} %bitcast.44, f32[384,32]{0,1:T(8,128)S(1)} %get-tuple-element.230, f32[32,256,384]{2,1,0:T(8,128)S(1)} %get-tuple-element.239, f32[384,32]{0,1:T(8,128)S(1)} %max.8, f32[384,256]{0,1:T(8,128)S(1)} %subtract_convert_fusion, f32[32]{0:T(128)S(1)} %get-tuple-element.141, ...), kind=kOutput, calls=%fused_computation.6 | convolution fusion | flops 830472192 | bytes 27853440 | tf_op jit(solution)/shard_map/while/body/eval_jaxpr/cond/branch_1_fun/qhk,khd->qhd/dot_general | solution.py:47
  154.9 2.7 %copy-done = f32[384,32,128]{2,0,1:T(8,128)} copy-done((f32[384,32,128]{2,0,1:T(8,128)}, f32[384,32,128]{2,0,1:T(8,128)S(1)}, u32[]{:S(2)}) %copy-start) | copy-done | bytes 6291480 | tf_op jit(solution)/shard_map/while/body/eval_jaxpr/cond
  157.5 2.5 fusion.25
  162.0 3.5 %collective-permute-start.7 = (f32[128,32,128]{2,0,1:T(8,128)S(1)}, f32[128,32,128]{2,0,1:T(8,128)S(1)}, u32[]{:S(2)}, u32[]{:S(2)}) collective-permute-start(f32[128,32,128]{2,0,1:T(8,128)S(1)} %get-tuple-element.243), channel_id=1, source_target_pairs={{0,8},{4,12},{8,16},{12,20},{16,24},{20,28},{24,32},{28,36},{32,40... | collective-permute-start | bytes 6291464 | tf_op jit(solution)/shard_map/ppermute | solution.py:14
  165.5 3.3 %collective-permute-start.2 = (f32[128,32]{0,1:T(8,128)S(1)}, f32[128,32]{0,1:T(8,128)S(1)}, u32[]{:S(2)}, u32[]{:S(2)}) collective-permute-start(f32[128,32]{0,1:T(8,128)S(1)} %get-tuple-element.246), channel_id=1, source_target_pairs={{0,4},{4,8},{8,12},{12,16},{16,20},{20,24},{24,28},{28,32},{32,36}... | collective-permute-start | bytes 49160 | tf_op jit(solution)/shard_map/ppermute | solution.py:14
  168.8 2.2 collective-permute-start.3
  171.0 3.5 %collective-permute-start.5 = (f32[128,32]{0,1:T(8,128)S(1)}, f32[128,32]{0,1:T(8,128)S(1)}, u32[]{:S(2)}, u32[]{:S(2)}) collective-permute-start(f32[128,32]{0,1:T(8,128)S(1)} %get-tuple-element.247), channel_id=1, source_target_pairs={{0,8},{4,12},{8,16},{12,20},{16,24},{20,28},{24,32},{28,36},{32,40... | collective-permute-start | bytes 49160 | tf_op jit(solution)/shard_map/ppermute | solution.py:14
  174.5 61.5 %collective-permute-done.2 = f32[128,32]{0,1:T(8,128)S(1)} collective-permute-done((f32[128,32]{0,1:T(8,128)S(1)}, f32[128,32]{0,1:T(8,128)S(1)}, u32[]{:S(2)}, u32[]{:S(2)}) %collective-permute-start.2) | collective-permute-done | bytes 16416 | tf_op jit(solution)/shard_map/ppermute | solution.py:14
  238.0 7.0 %collective-permute-done.6 = f32[128,32]{0,1:T(8,128)S(1)} collective-permute-done((f32[128,32]{0,1:T(8,128)S(1)}, f32[128,32]{0,1:T(8,128)S(1)}, u32[]{:S(2)}, u32[]{:S(2)}) %collective-permute-start.6) | collective-permute-done | bytes 16416 | tf_op jit(solution)/shard_map/ppermute | solution.py:14
  245.0 7.0 %copy_bitcast_fusion = bf16[128,4096]{1,0:T(8,128)(2,1)} fusion(f32[128,32]{0,1:T(8,128)S(1)} %get-tuple-element.233, f32[128,32,128]{2,0,1:T(8,128)S(1)} %collective-permute-done.7, f32[128,32]{0,1:T(8,128)S(1)} %get-tuple-element.237, f32[128,32]{0,1:T(8,128)S(1)} %get-tuple-element.236, f32[128,32,128]{2,0,1:T(8,128)S(1)} %collective-permute-done.4, ...), kind=kLoop, calls=%fused_computation.27 | loop fusion | flops 4194304 | bytes 7421952 | tf_op jit(solution)/shard_map/reshape | solution.py:169
  (63 shorter events, 9.8 us)
Async XLA Ops:
  6.5 100.2 %all-gather.2.cloned.1.call-start = ((), (), s32[]{:S(2)}) async-start(), calls=%async_computation.1 | async-start | bytes 5242880 | tf_op jit(solution)/shard_map/all_gather | solution.py:159
  10.4 7.6 %copy-start.3 = (bf16[128,4096]{1,0:T(8,128)(2,1)S(1)}, bf16[128,4096]{1,0:T(8,128)(2,1)}, u32[]{:S(2)}) copy-start(bf16[128,4096]{1,0:T(8,128)(2,1)} %param.9) | copy-start | bytes 3145732
  13.1 12.9 %copy-start.6 = (s32[128]{0:T(128)S(1)}, s32[128]{0:T(128)}, u32[]{:S(2)}) copy-start(s32[128]{0:T(128)} %param.12) | copy-start | bytes 1540
  13.1 87.8 %all-to-all-start = ((bf16[4,128,32,128]{3,2,1,0:T(8,128)(2,1)}), bf16[4,128,32,128]{3,2,1,0:T(8,128)(2,1)}, u32[]{:S(2)}, u32[]{:S(2)}) async-start(bf16[4,128,32,128]{3,2,1,0:T(8,128)(2,1)} %stack.3), calls=%async_computation | async-start | bytes 8388608 | tf_op jit(solution)/shard_map/all_to_all | solution.py:143
  18.8 25.4 %copy-start.1 = (bf16[128,4096]{0,1:T(8,128)(2,1)}, bf16[128,4096]{0,1:T(8,128)(2,1)S(1)}, u32[]{:S(2)}) copy-start(bf16[128,4096]{0,1:T(8,128)(2,1)S(1)} %copy.25) | copy-start | bytes 3145732
  18.8 25.4 %collective-permute-start = (bf16[128,32,128]{0,2,1:T(8,128)(2,1)S(1)}, bf16[128,32,128]{0,2,1:T(8,128)(2,1)S(1)}, u32[]{:S(2)}, u32[]{:S(2)}) collective-permute-start(bf16[128,32,128]{0,2,1:T(8,128)(2,1)S(1)} %bitcast.48), channel_id=1, source_target_pairs={{4,0},{8,4},{12,8},{16,12},{20,16},{24,20},{28,24},{32,28},{36,32}... | collective-permute-start | bytes 3145736 | tf_op jit(solution)/shard_map/ppermute | solution.py:14
  22.7 34.9 %collective-permute-start.1 = (bf16[128,32,128]{0,2,1:T(8,128)(2,1)S(1)}, bf16[128,32,128]{0,2,1:T(8,128)(2,1)}, u32[]{:S(2)}, u32[]{:S(2)}) collective-permute-start(bf16[128,32,128]{0,2,1:T(8,128)(2,1)S(1)} %bitcast.49), channel_id=1, source_target_pairs={{8,0},{12,4},{16,8},{20,12},{24,16},{28,20},{32,24},{36,28},{40,32... | collective-permute-start | bytes 3145736 | tf_op jit(solution)/shard_map/ppermute | solution.py:14
  44.1 1.0 copy-start.4
  106.8 9.4 %copy-start.2 = (bf16[384,32,128]{2,0,1:T(8,128)(2,1)S(1)}, bf16[384,32,128]{2,0,1:T(8,128)(2,1)}, u32[]{:S(2)}) copy-start(bf16[384,32,128]{2,0,1:T(8,128)(2,1)} %copy.27) | copy-start | bytes 9437188
  106.8 9.4 %copy-start.5 = (f32[32]{0:T(128)S(1)}, f32[32]{0:T(128)}, u32[]{:S(2)}) copy-start(f32[32]{0:T(128)} %param.13) | copy-start | bytes 388
  117.7 9.0 %slice-start = ((s8[6291456]{0:T(1024)(128)(4,1)}), s8[4194304]{0:T(1024)(128)(4,1)S(1)}, s32[]{:S(2)}) async-start(s8[6291456]{0:T(1024)(128)(4,1)} %bitcast.43), calls=%async_computation.2 | async-start | bytes 8388608 | tf_op jit(solution)/shard_map/while/body/eval_jaxpr/cond
  117.8 8.9 %slice-start.1 = ((s8[6291456]{0:T(1024)(128)(4,1)}), s8[2097152]{0:T(1024)(128)(4,1)S(1)}, s32[]{:S(2)}) async-start(s8[6291456]{0:T(1024)(128)(4,1)} %bitcast.43), calls=%async_computation.3 | async-start | bytes 4194304 | tf_op jit(solution)/shard_map/while/body/eval_jaxpr/cond
  134.2 2.7 %copy-start = (f32[384,32,128]{2,0,1:T(8,128)}, f32[384,32,128]{2,0,1:T(8,128)S(1)}, u32[]{:S(2)}) copy-start(f32[384,32,128]{2,0,1:T(8,128)S(1)} %bitcast_add_fusion) | copy-start | bytes 18874372 | tf_op jit(solution)/shard_map/while/body/eval_jaxpr/cond
  138.4 9.0 %slice-start = ((s8[6291456]{0:T(1024)(128)(4,1)}), s8[4194304]{0:T(1024)(128)(4,1)S(1)}, s32[]{:S(2)}) async-start(s8[6291456]{0:T(1024)(128)(4,1)} %bitcast.43), calls=%async_computation.2 | async-start | bytes 8388608 | tf_op jit(solution)/shard_map/while/body/eval_jaxpr/cond
  138.5 8.9 %slice-start.1 = ((s8[6291456]{0:T(1024)(128)(4,1)}), s8[2097152]{0:T(1024)(128)(4,1)S(1)}, s32[]{:S(2)}) async-start(s8[6291456]{0:T(1024)(128)(4,1)} %bitcast.43), calls=%async_computation.3 | async-start | bytes 4194304 | tf_op jit(solution)/shard_map/while/body/eval_jaxpr/cond
  154.9 2.7 %copy-start = (f32[384,32,128]{2,0,1:T(8,128)}, f32[384,32,128]{2,0,1:T(8,128)S(1)}, u32[]{:S(2)}) copy-start(f32[384,32,128]{2,0,1:T(8,128)S(1)} %bitcast_add_fusion) | copy-start | bytes 18874372 | tf_op jit(solution)/shard_map/while/body/eval_jaxpr/cond
  160.0 84.9 %collective-permute-start.4 = (f32[128,32,128]{2,0,1:T(8,128)S(1)}, f32[128,32,128]{2,0,1:T(8,128)S(1)}, u32[]{:S(2)}, u32[]{:S(2)}) collective-permute-start(f32[128,32,128]{2,0,1:T(8,128)S(1)} %get-tuple-element.242), channel_id=1, source_target_pairs={{0,4},{4,8},{8,12},{12,16},{16,20},{20,24},{24,28},{28,32},{32,36}... | collective-permute-start | bytes 6291464 | tf_op jit(solution)/shard_map/ppermute | solution.py:14
  162.0 83.0 %collective-permute-start.7 = (f32[128,32,128]{2,0,1:T(8,128)S(1)}, f32[128,32,128]{2,0,1:T(8,128)S(1)}, u32[]{:S(2)}, u32[]{:S(2)}) collective-permute-start(f32[128,32,128]{2,0,1:T(8,128)S(1)} %get-tuple-element.243), channel_id=1, source_target_pairs={{0,8},{4,12},{8,16},{12,20},{16,24},{20,28},{24,32},{28,36},{32,40... | collective-permute-start | bytes 6291464 | tf_op jit(solution)/shard_map/ppermute | solution.py:14
  165.5 70.5 %collective-permute-start.2 = (f32[128,32]{0,1:T(8,128)S(1)}, f32[128,32]{0,1:T(8,128)S(1)}, u32[]{:S(2)}, u32[]{:S(2)}) collective-permute-start(f32[128,32]{0,1:T(8,128)S(1)} %get-tuple-element.246), channel_id=1, source_target_pairs={{0,4},{4,8},{8,12},{12,16},{16,20},{20,24},{24,28},{28,32},{32,36}... | collective-permute-start | bytes 49160 | tf_op jit(solution)/shard_map/ppermute | solution.py:14
  168.8 69.1 %collective-permute-start.3 = (f32[128,32]{0,1:T(8,128)S(1)}, f32[128,32]{0,1:T(8,128)S(1)}, u32[]{:S(2)}, u32[]{:S(2)}) collective-permute-start(f32[128,32]{0,1:T(8,128)S(1)} %get-tuple-element.245), channel_id=1, source_target_pairs={{0,4},{4,8},{8,12},{12,16},{16,20},{20,24},{24,28},{28,32},{32,36}... | collective-permute-start | bytes 49160 | tf_op jit(solution)/shard_map/ppermute | solution.py:14
  171.0 66.9 %collective-permute-start.5 = (f32[128,32]{0,1:T(8,128)S(1)}, f32[128,32]{0,1:T(8,128)S(1)}, u32[]{:S(2)}, u32[]{:S(2)}) collective-permute-start(f32[128,32]{0,1:T(8,128)S(1)} %get-tuple-element.247), channel_id=1, source_target_pairs={{0,8},{4,12},{8,16},{12,20},{16,24},{20,28},{24,32},{28,36},{32,40... | collective-permute-start | bytes 49160 | tf_op jit(solution)/shard_map/ppermute | solution.py:14
  236.0 8.9 %collective-permute-start.6 = (f32[128,32]{0,1:T(8,128)S(1)}, f32[128,32]{0,1:T(8,128)S(1)}, u32[]{:S(2)}, u32[]{:S(2)}) collective-permute-start(f32[128,32]{0,1:T(8,128)S(1)} %get-tuple-element.244), channel_id=1, source_target_pairs={{0,8},{4,12},{8,16},{12,20},{16,24},{20,28},{24,32},{28,36},{32,40... | collective-permute-start | bytes 49160 | tf_op jit(solution)/shard_map/ppermute | solution.py:14
Sparse Core Ops, SparseCore 0:
  9.5 88.8 all-gather.1
